TPU v7x, 32 devices: a whole 2x2x4 slice. The times are simulated.
32 devices in a mesh: own: 4 (over y, x), dp: 8 (over z, core).
Axes of the slice: x: 2, y: 2, z: 4, core: 2. Of those that a mesh axis runs over, the one named last changes fastest.
Arguments:
- tokens: bfloat16 [8192, 1536], P('dp'), may hold values from -6 to 6
- assign: int32 [64, 2], P('dp'), may hold values from 0 to 7, all different within a row; in each aligned block of 8 rows (0 to 7, 8 to 15, ...) at most 5 rows name the same one
- gates: float32 [8192, 2], P('dp'), may hold values from 0.25 to 1
- cot: bfloat16 [8192, 1536], P('dp', 'own'), may hold values from -1.75 to 1.75
- w_in: bfloat16 [8, 1536, 2048], P('own', None, 'dp'), may hold values from -0.15625 to 0.15625
- w_out: bfloat16 [8, 2048, 1536], P('own', 'dp'), may hold values from -0.125 to 0.125
Outputs:
- mixed: bfloat16 [8192, 1536], P('dp', 'own')
- grad_tokens: bfloat16 [8192, 1536], P('dp', 'own')
- grad_w_in: float32 [8, 1536, 2048], P('own', None, 'dp')
- grad_w_out: float32 [8, 2048, 1536], P('own', 'dp')
Inputs may be any that keep to these rules, and one draw needn't show every extreme that they name: `assign`: the two entries of a block name different experts. Among the 8 blocks of one index of dp no expert is named more than 5 times, and in every draw some expert is named exactly 5 times by the blocks of some index of dp.
All inputs are finite; a program needn't handle non-finite values.
Results may differ from a plain program's by a relative error of at most 0.012.
Values may be sent and summed in bfloat16 or wider, within the bound.
A program may use at most 128 MiB of HBM per device.

v0:
```python
import jax
import jax.numpy as jnp
from jax import lax
from jax.sharding import PartitionSpec as P

CAP = 5


def pick_blocks(assign_rows, expert, capacity):
    hit_flag = jnp.logical_or(assign_rows[:, 0] == expert, assign_rows[:, 1] == expert).astype(
        jnp.int32
    )
    slot_rank = jnp.cumsum(hit_flag) - 1
    slot_ids = jnp.arange(capacity, dtype=jnp.int32)
    matches = jnp.logical_and(
        hit_flag[None, :] == 1, slot_rank[None, :] == slot_ids[:, None]
    ).astype(jnp.int32)
    where_idx = jnp.arange(assign_rows.shape[0], dtype=jnp.int32)
    blocks = jnp.sum(matches * where_idx[None, :], axis=1)
    is_valid = jnp.sum(matches, axis=1).astype(jnp.float32)
    return (blocks, is_valid)


def block_gates(assign_rows, gate_blocks, blocks, is_valid, expert):
    chosen = assign_rows[blocks]
    picked_gates = gate_blocks[blocks]
    first_hit = (chosen[:, 0] == expert).astype(jnp.float32)
    second_hit = (chosen[:, 1] == expert).astype(jnp.float32)
    mixing = picked_gates[..., 0] * first_hit[:, None] + picked_gates[..., 1] * second_hit[:, None]
    return mixing * is_valid[:, None]


def gelu_cdf(values):
    return 0.5 * (1.0 + jax.scipy.special.erf(values * 0.7071067811865476))


def gelu_slope(values):
    return gelu_cdf(values) + values * jnp.exp(-0.5 * values * values) * 0.3989422804014327


def place_rows(terms, blocks, block_count):
    block_len = terms.shape[-2]
    width = terms.shape[-1]
    zeros = jnp.zeros((block_count, block_len, width), jnp.float32)
    placed = zeros.at[blocks.reshape(-1)].add(terms.reshape(-1, block_len, width))
    return placed.reshape(block_count * block_len, width)


def body(tokens, assign, gates, cot, w_in, w_out):
    own_count = w_in.shape[0]
    block_count = assign.shape[0]
    block_len = tokens.shape[0] // block_count
    width = tokens.shape[1]
    full_in, full_out = (
        lax.all_gather(w_in, "dp", axis=2, tiled=True),
        lax.all_gather(w_out, "dp", axis=1, tiled=True),
    )
    expert_ids = lax.axis_index("own") * own_count + jnp.arange(own_count, dtype=jnp.int32)
    blocks, is_valid = jax.vmap(pick_blocks, (None, 0, None))(assign, expert_ids, CAP)
    gate_blocks = gates.reshape(block_count, block_len, 2)
    mixing = jax.vmap(block_gates, (None, None, 0, 0, 0))(
        assign, gate_blocks, blocks, is_valid, expert_ids
    )
    weight_rows = mixing.reshape(own_count, CAP * block_len)
    token_blocks = tokens.reshape(block_count, block_len, width)
    picked = token_blocks[blocks].reshape(own_count, CAP * block_len, width)
    pre_act = jnp.einsum("erd,edf->erf", picked, full_in, preferred_element_type=jnp.float32)
    hidden = (pre_act * gelu_cdf(pre_act)).astype(jnp.bfloat16)
    expert_out = jnp.einsum("erf,efd->erd", hidden, full_out, preferred_element_type=jnp.float32)
    contrib = (weight_rows[..., None] * expert_out).reshape(own_count, CAP, block_len, width)
    partial_rows = place_rows(contrib, blocks, block_count)
    mixed = lax.psum_scatter(
        partial_rows.astype(jnp.bfloat16), "own", scatter_dimension=1, tiled=True
    )
    cot_full = lax.all_gather(cot, "own", axis=1, tiled=True)
    cot_picked = cot_full.reshape(block_count, block_len, width)[blocks].reshape(
        own_count, CAP * block_len, width
    )
    grad_out = (weight_rows[..., None] * cot_picked.astype(jnp.float32)).astype(jnp.bfloat16)
    grad_hidden = jnp.einsum("erd,efd->erf", grad_out, full_out, preferred_element_type=jnp.float32)
    grad_pre = (grad_hidden * gelu_slope(pre_act)).astype(jnp.bfloat16)
    grad_in_terms = jnp.einsum(
        "erf,edf->erd", grad_pre, full_in, preferred_element_type=jnp.float32
    )
    grad_rows = place_rows(
        grad_in_terms.reshape(own_count, CAP, block_len, width), blocks, block_count
    )
    grad_tokens = lax.psum_scatter(
        grad_rows.astype(jnp.bfloat16), "own", scatter_dimension=1, tiled=True
    )
    out_full = jnp.einsum("erf,erd->efd", hidden, grad_out, preferred_element_type=jnp.float32)
    in_full = jnp.einsum("erf,erd->efd", grad_pre, picked, preferred_element_type=jnp.float32)
    grad_w_out, in_shard = (
        lax.psum_scatter(
            out_full.astype(jnp.bfloat16), "dp", scatter_dimension=1, tiled=True
        ).astype(jnp.float32),
        lax.psum_scatter(
            in_full.astype(jnp.bfloat16), "dp", scatter_dimension=1, tiled=True
        ).astype(jnp.float32),
    )
    grad_w_in = jnp.transpose(in_shard, (0, 2, 1))
    return (mixed, grad_tokens, grad_w_in, grad_w_out)


def solution(mesh):
    placed = (
        P("dp", None),
        P("dp", None),
        P("dp", None),
        P("dp", "own"),
        P("own", None, "dp"),
        P("own", "dp", None),
    )
    return jax.shard_map(
        body,
        mesh=mesh,
        in_specs=placed,
        out_specs=(P("dp", "own"), P("dp", "own"), P("own", None, "dp"), P("own", "dp", None)),
        check_vma=False,
    )
```

profile of v0, /device:TPU:0, one launch (start us, length us, event | category | flops | bytes accessed | tf_op | source)
XLA Modules:
  0.0 712.9 jit_solution(11356649199998940903)
XLA Ops:
  7.2 0.0 copy-start
  7.2 0.0 all-gather.8.cloned.1.call-start
  7.2 0.7 all-gather.8.cloned.1.call-update
  7.9 0.0 all-gather.4.cloned.1.call-start
  8.0 0.7 all-gather.4.cloned.1.call-update
  8.7 0.0 all-gather.6.cloned.1.call-start
  8.7 0.7 all-gather.6.cloned.1.call-update
  9.4 0.0 reduce-scatter.15.cloned.1.call-start
  9.5 0.8 copy.27
  10.2 0.8 slice_bitcast_fusion.1
  11.0 0.1 broadcast_compare_fusion
  11.0 0.2 reduce_window_sum.11
  11.2 0.3 convert_reduce_fusion
  11.5 0.1 copy.25
  11.6 0.1 reshape.231
  11.7 0.1 reshape.241
  11.8 0.6 gather_fusion.1
  12.3 0.1 copy.28
  12.4 0.1 reshape.248
  12.5 1.3 gather_fusion
  13.8 0.1 copy.29
  13.9 0.0 copy-done
  13.9 2.9 gather_fusion.2
  16.8 0.1 fusion.8
  16.9 0.1 broadcast_bitcast_fusion
  17.0 0.1 broadcast_bitcast_fusion.1
  17.1 39.4 %all-gather.8.cloned.1.call-done = bf16[1024,1536]{1,0:T(8,128)(2,1)} async-done(((bf16[1024,384]{1,0:T(8,128)(2,1)}), bf16[1024,1536]{1,0:T(8,128)(2,1)}) %all-gather.8.cloned.1.call-update) | async-done | bytes 3145744 | tf_op jit(solution)/shard_map/all_gather | solution.py:75
  56.4 4.8 gather_fusion.3
  61.3 4.7 fusion.6
  65.9 109.3 %all-gather.4.cloned.1.call-done = bf16[2,1536,2048]{2,1,0:T(8,128)(2,1)} async-done(((bf16[2,1536,256]{2,1,0:T(8,128)(2,1)}), bf16[2,1536,2048]{2,1,0:T(8,128)(2,1)}) %all-gather.4.cloned.1.call-update) | async-done | bytes 12582928 | tf_op jit(solution)/shard_map/all_gather | solution.py:55
  175.2 16.1 %multiply_convert_fusion = (bf16[2,640,2048]{2,1,0:T(8,128)(2,1)}, f32[2,640,2048]{2,1,0:T(8,128)}) fusion(bf16[2,640,1536]{2,1,0:T(8,128)(2,1)} %bitcast.82, bf16[2,1536,2048]{2,1,0:T(8,128)(2,1)} %all-gather.4.cloned.1.call-done), kind=kOutput, calls=%fused_computation.15 | convolution fusion | flops 8066170880 | bytes 32243712 | tf_op jit(solution)/shard_map/erd,edf->erf/dot_general | solution.py:67
  191.3 100.5 %all-gather.6.cloned.1.call-done = bf16[2,2048,1536]{2,1,0:T(8,128)(2,1)} async-done(((bf16[2,256,1536]{2,1,0:T(8,128)(2,1)}), bf16[2,2048,1536]{2,1,0:T(8,128)(2,1)}) %all-gather.6.cloned.1.call-update) | async-done | bytes 12582928 | tf_op jit(solution)/shard_map/all_gather | solution.py:56
  291.8 17.5 %fusion.5 = bf16[2,640,2048]{2,1,0:T(8,128)(2,1)} fusion(f32[2,640,2048]{2,1,0:T(8,128)} %get-tuple-element.31, bf16[2,640,1536]{2,1,0:T(8,128)(2,1)} %fusion.6, bf16[2,2048,1536]{2,1,0:T(8,128)(2,1)} %all-gather.6.cloned.1.call-done), kind=kOutput, calls=%fused_computation.14 | convolution fusion | flops 8079278080 | bytes 32243712 | tf_op jit(solution)/shard_map/erd,efd->erf/dot_general | solution.py:80
  309.3 14.8 %fusion.11 = f32[2,640,1536]{2,1,0:T(8,128)} fusion(bf16[2,640,2048]{2,1,0:T(8,128)(2,1)} %fusion.5, bf16[2,1536,2048]{2,1,0:T(8,128)(2,1)} %all-gather.4.cloned.1.call-done), kind=kOutput, calls=%fused_computation.47 | convolution fusion | flops 8053063680 | bytes 25690112 | tf_op jit(solution)/shard_map/erf,edf->erd/dot_general | solution.py:82
  324.1 3.4 broadcast.143.clone.1
  327.5 17.6 %scatter_fusion.1 = f32[8,128,1536]{2,1,0:T(8,128)} fusion(f32[8,128,1536]{2,1,0:T(8,128)} %broadcast.143.clone.1, s32[10]{0:T(128)S(1)} %fusion.10, f32[10,128,1536]{2,1,0:T(8,128)} %bitcast.80), kind=kCustom, calls=%fused_computation.5 | custom fusion | flops 1966080 | bytes 23593000 | tf_op jit(solution)/shard_map/scatter-add | solution.py:45
  345.1 3.2 convert_element_type.72
  348.3 3.1 copy.37
  351.4 0.0 reduce-scatter.15.cloned.1.call-update
  351.4 0.0 reduce-scatter.13.cloned.1.call-start
  351.5 14.8 %convolution_multiply_fusion = f32[2,640,1536]{2,1,0:T(8,128)} fusion(bf16[2,640,2048]{2,1,0:T(8,128)(2,1)} %get-tuple-element.30, bf16[2,2048,1536]{2,1,0:T(8,128)(2,1)} %all-gather.6.cloned.1.call-done, f32[2,640]{1,0:T(2,128)S(1)} %bitcast_multiply_fusion), kind=kOutput, calls=%fused_computation.19 | convolution fusion | flops 8055029760 | bytes 25695232 | tf_op jit(solution)/shard_map/erf,efd->erd/dot_general | solution.py:69
  366.2 3.5 broadcast.143.clone
  369.7 18.0 %scatter_fusion = f32[8,128,1536]{2,1,0:T(8,128)} fusion(f32[8,128,1536]{2,1,0:T(8,128)} %broadcast.143.clone, s32[10]{0:T(128)S(1)} %fusion.10, f32[10,128,1536]{2,1,0:T(8,128)} %bitcast.79), kind=kCustom, calls=%fused_computation.4 | custom fusion | flops 1966080 | bytes 23593000 | tf_op jit(solution)/shard_map/scatter-add | solution.py:45
  387.7 3.2 convert_element_type.66
  390.9 2.9 copy.35
  393.8 0.0 reduce-scatter.13.cloned.1.call-update
  393.8 0.0 reduce-scatter.9.cloned.1.call-start
  393.9 15.8 %convolution_convert_fusion.1 = bf16[2,2048,1536]{2,1,0:T(8,128)(2,1)} fusion(bf16[2,640,2048]{2,1,0:T(8,128)(2,1)} %fusion.5, bf16[2,640,1536]{2,1,0:T(8,128)(2,1)} %bitcast.83), kind=kOutput, calls=%fused_computation.8 | convolution fusion | flops 8059355136 | bytes 21757952 | tf_op jit(solution)/shard_map/erf,erd->efd/dot_general | solution.py:92
  409.6 0.0 reduce-scatter.9.cloned.1.call-update
  409.7 0.0 reduce-scatter.11.cloned.1.call-start
  409.7 16.2 %convolution_convert_fusion = bf16[2,2048,1536]{2,1,0:T(8,128)(2,1)} fusion(bf16[2,640,2048]{2,1,0:T(8,128)(2,1)} %get-tuple-element.30, bf16[2,640,1536]{2,1,0:T(8,128)(2,1)} %fusion.6), kind=kOutput, calls=%fused_computation.7 | convolution fusion | flops 8059355136 | bytes 21757952 | tf_op jit(solution)/shard_map/erf,erd->efd/dot_general | solution.py:91
  425.9 0.0 reduce-scatter.11.cloned.1.call-update
  425.9 0.0 reduce-scatter.15.cloned.1.call-done
  425.9 2.3 copy.38
  428.2 13.1 %reduce-scatter.13.cloned.1.call-done = bf16[384,1024]{1,0:T(8,128)(2,1)} async-done(((bf16[1536,1024]{1,0:T(8,128)(2,1)}), bf16[384,1024]{1,0:T(8,128)(2,1)}) %reduce-scatter.13.cloned.1.call-update) | async-done | bytes 786448
  441.3 2.3 copy.36
  443.6 129.1 %reduce-scatter.9.cloned.1.call-done = bf16[2,256,1536]{2,1,0:T(8,128)(2,1)} async-done(((bf16[2,2048,1536]{2,1,0:T(8,128)(2,1)}), bf16[2,256,1536]{2,1,0:T(8,128)(2,1)}) %reduce-scatter.9.cloned.1.call-update) | async-done | bytes 1572880 | tf_op jit(solution)/shard_map/reduce_scatter | solution.py:97
  572.7 0.0 copy-start.1
  572.7 3.6 convert_bitcast_fusion
  576.3 3.9 copy.32
  580.2 122.4 %reduce-scatter.11.cloned.1.call-done = bf16[2,256,1536]{2,1,0:T(8,128)(2,1)} async-done(((bf16[2,2048,1536]{2,1,0:T(8,128)(2,1)}), bf16[2,256,1536]{2,1,0:T(8,128)(2,1)}) %reduce-scatter.11.cloned.1.call-update) | async-done | bytes 1572880 | tf_op jit(solution)/shard_map/reduce_scatter | solution.py:94
  702.6 3.5 convert_element_type.76
  706.1 0.0 copy-done.1
  (8 shorter events, 0.1 us)
Async XLA Ops:
  7.2 6.7 copy-start
  7.2 49.3 %all-gather.8.cloned.1.call-start = ((), (), s32[]{:S(2)}) async-start(), calls=%async_computation.6 | async-start | bytes 3932160 | tf_op jit(solution)/shard_map/all_gather | solution.py:75
  7.9 167.3 %all-gather.4.cloned.1.call-start = ((), (), s32[]{:S(2)}) async-start(), calls=%async_computation.4 | async-start | bytes 14155776 | tf_op jit(solution)/shard_map/all_gather | solution.py:55
  8.7 283.1 %all-gather.6.cloned.1.call-start = ((), (), s32[]{:S(2)}) async-start(), calls=%async_computation.5 | async-start | bytes 14155776 | tf_op jit(solution)/shard_map/all_gather | solution.py:56
  9.4 416.5 %reduce-scatter.15.cloned.1.call-start = ((), (), s32[]{:S(2)}) async-start(), calls=%async_computation.10 | async-start | bytes 3932160
  351.4 89.9 %reduce-scatter.13.cloned.1.call-start = ((), (), s32[]{:S(2)}) async-start(), calls=%async_computation.9 | async-start | bytes 3932160
  393.8 178.9 %reduce-scatter.9.cloned.1.call-start = ((), (), s32[]{:S(2)}) async-start(), calls=%async_computation.7 | async-start | bytes 14155776 | tf_op jit(solution)/shard_map/reduce_scatter | solution.py:97
  409.7 292.9 %reduce-scatter.11.cloned.1.call-start = ((), (), s32[]{:S(2)}) async-start(), calls=%async_computation.8 | async-start | bytes 14155776 | tf_op jit(solution)/shard_map/reduce_scatter | solution.py:94
  572.7 133.4 %copy-start.1 = (bf16[1024,1536]{1,0:T(8,128)(2,1)S(1)}, bf16[1024,1536]{1,0:T(8,128)(2,1)}, u32[]{:S(2)}) copy-start(bf16[1024,1536]{1,0:T(8,128)(2,1)} %param.6) | copy-start | bytes 9437188
Sparse Core Ops, SparseCore 0:
  9.8 46.5 all-gather.7
  58.0 117.1 all-gather.3
  176.8 114.9 all-gather.5
  351.5 42.3 reduce-scatter.14
  397.3 43.9 reduce-scatter.12
  443.5 129.1 reduce-scatter.8
  575.0 127.5 reduce-scatter.10
where the time goes:
time: 714 us; the launch traced here: 713 us
  waiting for transfers between devices  516 us (72%)
  matrix products  95.1 us (13%)
  other arithmetic  54.4 us (8%)
  local copies, waits for them, and re-layouts  33 us (5%)
  between operations  14.2 us (2%)
    reduce_scatter x1, waiting for transfers between devices, body(): lax.psum_scatter(in_full.astype(jnp.bfloat16), 'dp', scatter_dimension=1,...  129 us
    reduce_scatter x1, waiting for transfers between devices, body(): lax.psum_scatter(out_full.astype(jnp.bfloat16), 'dp', scatter_dimension=1...  122 us
    all_gather x1, waiting for transfers between devices, body(): lax.all_gather(w_in, 'dp', axis=2, tiled=True)  109 us
    all_gather x1, waiting for transfers between devices, body(): lax.all_gather(w_out, 'dp', axis=1, tiled=True)  100 us
    all_gather x1, waiting for transfers between devices, body(): cot_full = lax.all_gather(cot, 'own', axis=1, tiled=True)  39.4 us
    scatter-add x2, other arithmetic, place_rows(): zeros.at[blocks.reshape(-1)].add(terms.reshape(-1, block_len, width))  35.7 us
    dot_general x1, matrix products, body(): jnp.einsum('erd,efd->erf', grad_out, full_out, preferred_element_type=jnp...  17.5 us
    dot_general x1, matrix products, body(): jnp.einsum('erf,erd->efd', hidden, grad_out, preferred_element_type=jnp.f...  16.2 us
  transfers between devices with their start and end apart: 7, of which 6 were waited for; matrix products, arithmetic and copies ran while one was open for 17% of the time, Pallas kernels for 0%

commit v1 on v0

--- a/solution.py
+++ b/solution.py
@@ -1,9 +1,14 @@
+import functools
+
 import jax
 import jax.numpy as jnp
 from jax import lax
+from jax.experimental import pallas as pl
+from jax.experimental.pallas import tpu as pltpu
 from jax.sharding import PartitionSpec as P
 
 CAP = 5
+MESH = pl.DeviceIdType.MESH
 
 
 def pick_blocks(assign_rows, expert, capacity):
@@ -18,7 +23,7 @@
     where_idx = jnp.arange(assign_rows.shape[0], dtype=jnp.int32)
     blocks = jnp.sum(matches * where_idx[None, :], axis=1)
     is_valid = jnp.sum(matches, axis=1).astype(jnp.float32)
-    return (blocks, is_valid)
+    return (blocks, is_valid, hit_flag, slot_rank)
 
 
 def block_gates(assign_rows, gate_blocks, blocks, is_valid, expert):
@@ -30,6 +35,377 @@
     return mixing * is_valid[:, None]
 
 
+def expert_kernel(
+    chips,
+    x_ref,
+    g_ref,
+    wt_ref,
+    own_w,
+    y_out,
+    gx_out,
+    dw_out,
+    w_all,
+    h_all,
+    p_all,
+    sums,
+    stage,
+    ag_send,
+    ag_recv,
+    rs_send,
+    rs_recv,
+    own_sem,
+    out_sem,
+):
+    me = lax.axis_index("dp")
+    chip = me // 2
+    rows, width = x_ref.shape
+    depth = own_w.shape[1] // 2
+    last = chips - 1
+    has_left, has_right = chip > 0, chip < last
+
+    def at_chunk(ref, q):
+        return ref.at[:, pl.ds(pl.multiple_of(q * depth, depth), depth)]
+
+    def gather_copy(q, way):
+        return pltpu.make_async_remote_copy(
+            src_ref=at_chunk(w_all, q),
+            dst_ref=at_chunk(w_all, q),
+            send_sem=ag_send.at[q, (way + 1) // 2],
+            recv_sem=ag_recv.at[q],
+            device_id={"dp": me + 2 * way},
+            device_id_type=MESH,
+        )
+
+    def sum_copy(slot, way):
+        return pltpu.make_async_remote_copy(
+            src_ref=sums.at[slot],
+            dst_ref=sums.at[slot],
+            send_sem=rs_send.at[slot],
+            recv_sem=rs_recv.at[slot],
+            device_id={"dp": me + 2 * way},
+            device_id_type=MESH,
+        )
+
+    own_copy = pltpu.make_async_copy(
+        own_w, w_all.at[:, pl.ds(pl.multiple_of(chip * 2 * depth, depth), 2 * depth)], own_sem
+    )
+    own_copy.start()
+    barrier = pltpu.get_barrier_semaphore()
+
+    @pl.when(has_left)
+    def _():
+        pl.semaphore_signal(barrier, inc=1, device_id={"dp": me - 2}, device_id_type=MESH)
+
+    @pl.when(has_right)
+    def _():
+        pl.semaphore_signal(barrier, inc=1, device_id={"dp": me + 2}, device_id_type=MESH)
+
+    pl.semaphore_wait(barrier, has_left.astype(jnp.int32) + has_right.astype(jnp.int32))
+
+    own_copy.wait()
+    for sub in range(2):
+
+        @pl.when(has_left)
+        def _():
+            gather_copy(2 * chip + sub, -1).start()
+
+        @pl.when(has_right)
+        def _():
+            gather_copy(2 * chip + sub, 1).start()
+
+    tile = rows // 2
+    nt = (((1,), (1,)), ((), ()))
+
+    def activate(q):
+        cols = pl.ds(pl.multiple_of(q * depth, depth), depth)
+
+        def step(r, carry):
+            part = pl.ds(pl.multiple_of(r * tile, tile), tile)
+            pre = lax.dot_general(
+                x_ref[part, :], w_all[0, cols, :], nt, preferred_element_type=jnp.float32
+            )
+            grad_hidden = lax.dot_general(
+                g_ref[part, :], w_all[1, cols, :], nt, preferred_element_type=jnp.float32
+            )
+            cdf = 0.5 * (1.0 + lax.erf(pre * 0.7071067811865476))
+            slope = cdf + pre * jnp.exp(-0.5 * pre * pre) * 0.3989422804014327
+            h_all[part, cols] = (pre * cdf).astype(jnp.bfloat16)
+            p_all[part, cols] = (grad_hidden * slope).astype(jnp.bfloat16)
+            return carry
+
+        lax.fori_loop(0, 2, step, 0)
+
+    piece = width // 3
+
+    def weight_grads(q, emit):
+        cols = pl.ds(pl.multiple_of(q * depth, depth), depth)
+        for kind, left, right in ((0, p_all, x_ref), (1, h_all, g_ref)):
+            turned = left[:, cols].T
+
+            def step(k, carry):
+                span = pl.ds(pl.multiple_of(k * piece, piece), piece)
+                emit(
+                    kind,
+                    span,
+                    jnp.dot(turned, right[:, span], preferred_element_type=jnp.float32),
+                )
+                return carry
+
+            lax.fori_loop(0, 3, step, 0)
+
+    def add_and_send(q, slot, way, fed):
+        @pl.when(fed)
+        def _():
+            sum_copy(slot, way).wait_recv()
+
+        @pl.when(jnp.logical_not(fed))
+        def _():
+            sums[slot] = jnp.zeros(sums.shape[1:], sums.dtype)
+
+        def emit(kind, span, value):
+            sums[slot, kind, :, span] = (
+                value + sums[slot, kind, :, span].astype(jnp.float32)
+            ).astype(jnp.bfloat16)
+
+        weight_grads(q, emit)
+        sum_copy(slot, way).start()
+
+    def chunk_of(n, way):
+        return 2 * (chip + way * (1 + n // 2)) + n % 2
+
+    count_left, count_right = 2 * chip, 2 * (last - chip)
+    lag_left, lag_right = 3 * (last - chip), 3 * chip
+
+    activate(2 * chip)
+    activate(2 * chip + 1)
+
+    turns = max([2 * p + 3 * (last - p) for p in range(1, chips)])
+
+    def turn(t, carry):
+        for way, count in ((-1, count_left), (1, count_right)):
+
+            @pl.when(t < count)
+            def _():
+                q = chunk_of(t, way)
+                gather_copy(q, way).wait_recv()
+
+                @pl.when(has_right if way == -1 else has_left)
+                def _():
+                    gather_copy(q, -way).start()
+
+                activate(q)
+
+        for way, count, lag in ((-1, count_left, lag_left), (1, count_right, lag_right)):
+            n = t - lag
+
+            @pl.when(jnp.logical_and(n >= 0, n < count))
+            def _():
+                q = chunk_of(n, way)
+                slot = q if way == -1 else q + 2
+                add_and_send(q, slot, way, has_right if way == -1 else has_left)
+
+        return carry
+
+    lax.fori_loop(0, turns, turn, 0)
+
+    out_tile = rows // 5
+
+    def rows_out(i, carry):
+        part = pl.ds(pl.multiple_of(i * out_tile, out_tile), out_tile)
+
+        def columns(k, inner):
+            span = pl.ds(pl.multiple_of(k * piece, piece), piece)
+            stage[0, :, span] = (
+                jnp.dot(h_all[part, :], w_all[1, :, span], preferred_element_type=jnp.float32)
+                * wt_ref[part, :]
+            ).astype(jnp.bfloat16)
+            stage[1, :, span] = jnp.dot(
+                p_all[part, :], w_all[0, :, span], preferred_element_type=jnp.float32
+            ).astype(jnp.bfloat16)
+            return inner
+
+        lax.fori_loop(0, 3, columns, 0)
+        y_copy = pltpu.make_async_copy(stage.at[0], y_out.at[part], out_sem.at[0])
+        gx_copy = pltpu.make_async_copy(stage.at[1], gx_out.at[part], out_sem.at[1])
+        y_copy.start()
+        gx_copy.start()
+        y_copy.wait()
+        gx_copy.wait()
+        return carry
+
+    lax.fori_loop(0, 5, rows_out, 0)
+
+    def finish(sub, carry):
+        q = 2 * chip + sub
+
+        @pl.when(has_left)
+        def _():
+            sum_copy(q + 2, 1).wait_recv()
+
+        @pl.when(has_right)
+        def _():
+            sum_copy(q, -1).wait_recv()
+
+        @pl.when(jnp.logical_not(has_left))
+        def _():
+            sums[q + 2] = jnp.zeros(sums.shape[1:], sums.dtype)
+
+        @pl.when(jnp.logical_not(has_right))
+        def _():
+            sums[q] = jnp.zeros(sums.shape[1:], sums.dtype)
+
+        def emit(kind, span, value):
+            dw_out[sub, kind, :, span] = (
+                value
+                + sums[q, kind, :, span].astype(jnp.float32)
+                + sums[q + 2, kind, :, span].astype(jnp.float32)
+            ).astype(jnp.bfloat16)
+
+        weight_grads(q, emit)
+        return carry
+
+    lax.fori_loop(0, 2, finish, 0)
+
+    for sub in range(2):
+
+        @pl.when(has_left)
+        def _():
+            gather_copy(2 * chip + sub, -1).wait_send()
+
+        @pl.when(has_right)
+        def _():
+            gather_copy(2 * chip + sub, 1).wait_send()
+
+    def drain(n, carry):
+        for way, count in ((-1, count_left), (1, count_right)):
+
+            @pl.when(n < count)
+            def _():
+                q = chunk_of(n, way)
+
+                @pl.when(has_right if way == -1 else has_left)
+                def _():
+                    gather_copy(q, -way).wait_send()
+
+                sum_copy(q if way == -1 else q + 2, way).wait_send()
+
+        return carry
+
+    lax.fori_loop(0, 2 * last, drain, 0)
+
+
+def run_experts(shards, x, g, weights, own_w):
+    chips = shards // 2
+    rows, width = x.shape
+    depth = own_w.shape[1] // 2
+    hidden = shards * depth
+    slots = shards + 2
+    vmem = pl.BlockSpec(memory_space=pltpu.VMEM)
+    hbm = pl.BlockSpec(memory_space=pl.ANY)
+    return pl.pallas_call(
+        functools.partial(expert_kernel, chips),
+        out_shape=(
+            jax.ShapeDtypeStruct((rows, width), jnp.bfloat16),
+            jax.ShapeDtypeStruct((rows, width), jnp.bfloat16),
+            jax.ShapeDtypeStruct((2, 2, depth, width), jnp.bfloat16),
+        ),
+        in_specs=[vmem, vmem, vmem, hbm],
+        out_specs=(hbm, hbm, vmem),
+        scratch_shapes=[
+            pltpu.VMEM((2, hidden, width), jnp.bfloat16),
+            pltpu.VMEM((rows, hidden), jnp.bfloat16),
+            pltpu.VMEM((rows, hidden), jnp.bfloat16),
+            pltpu.VMEM((slots, 2, depth, width), jnp.bfloat16),
+            pltpu.VMEM((2, rows // 5, width), jnp.bfloat16),
+            pltpu.SemaphoreType.DMA((shards, 2)),
+            pltpu.SemaphoreType.DMA((shards,)),
+            pltpu.SemaphoreType.DMA((slots,)),
+            pltpu.SemaphoreType.DMA((slots,)),
+            pltpu.SemaphoreType.DMA,
+            pltpu.SemaphoreType.DMA((2,)),
+        ],
+        compiler_params=pltpu.CompilerParams(
+            collective_id=0, has_side_effects=True, vmem_limit_bytes=62 * 1024 * 1024
+        ),
+        cost_estimate=pl.CostEstimate(
+            flops=12 * rows * width * hidden, bytes_accessed=30_000_000, transcendentals=0
+        ),
+    )(x, g, weights, own_w)
+
+
+def body(shards, tokens, assign, gates, cot, w_in, w_out):
+    own_count = w_in.shape[0]
+    if own_count != 2:
+        return plain_body(tokens, assign, gates, cot, w_in, w_out)
+    block_count = assign.shape[0]
+    block_len = tokens.shape[0] // block_count
+    width = tokens.shape[1]
+    rows = CAP * block_len
+    core = lax.axis_index("dp") % 2
+    pairs = [(i, i ^ 1) for i in range(shards)]
+
+    def swap(array):
+        return lax.ppermute(array, "dp", pairs)
+
+    def mine(array):
+        return lax.dynamic_index_in_dim(array, core, 0, keepdims=False)
+
+    def other(array):
+        return lax.dynamic_index_in_dim(array, 1 - core, 0, keepdims=False)
+
+    both = jnp.stack([jnp.transpose(w_in, (0, 2, 1)), w_out], axis=1)
+    kept, got = mine(both), swap(other(both))
+    own_w = jnp.where(
+        core == 0,
+        jnp.concatenate([kept, got], axis=1),
+        jnp.concatenate([got, kept], axis=1),
+    )
+    expert_ids = lax.axis_index("own") * own_count + jnp.arange(own_count, dtype=jnp.int32)
+    blocks, is_valid, hits, ranks = jax.vmap(pick_blocks, (None, 0, None))(assign, expert_ids, CAP)
+    gate_blocks = gates.reshape(block_count, block_len, 2)
+    mixing = jax.vmap(block_gates, (None, None, 0, 0, 0))(
+        assign, gate_blocks, blocks, is_valid, expert_ids
+    )
+    weight_rows = mixing.reshape(own_count, rows)
+    token_blocks = tokens.reshape(block_count, block_len, width)
+    picked = token_blocks[blocks].reshape(own_count, rows, width)
+    cot_full = lax.all_gather(cot, "own", axis=1, tiled=True)
+    cot_picked = cot_full.reshape(block_count, block_len, width)[blocks].reshape(
+        own_count, rows, width
+    )
+    grad_out = (weight_rows[..., None] * cot_picked.astype(jnp.float32)).astype(jnp.bfloat16)
+
+    def shared(array):
+        return jnp.concatenate([mine(array), swap(other(array))], axis=0)
+
+    x = shared(picked)
+    g = shared(grad_out)
+    weights = shared(weight_rows)[:, None]
+    y, gx, dw = run_experts(shards, x, g, weights, own_w)
+
+    my_hit, my_rank = mine(hits), mine(ranks)
+    other_hit, other_rank = other(hits), other(ranks)
+
+    def by_block(array):
+        def take(part, hit, rank):
+            chosen = part.reshape(CAP, block_len, width)[jnp.clip(rank, 0, CAP - 1)]
+            return jnp.where(hit[:, None, None] == 1, chosen.astype(jnp.float32), 0.0)
+
+        back = swap(array[rows:])
+        total = take(array[:rows], my_hit, my_rank) + take(back, other_hit, other_rank)
+        total = total.astype(jnp.bfloat16).reshape(block_count * block_len, width)
+        return lax.psum_scatter(total, "own", scatter_dimension=1, tiled=True)
+
+    mixed = by_block(y)
+    grad_tokens = by_block(gx)
+    dw_kept, dw_got = mine(dw), swap(other(dw))
+    dw_all = jnp.where(
+        core == 0, jnp.stack([dw_kept, dw_got]), jnp.stack([dw_got, dw_kept])
+    ).astype(jnp.float32)
+    grad_w_in = jnp.transpose(dw_all[:, 0], (0, 2, 1))
+    return (mixed, grad_tokens, grad_w_in, dw_all[:, 1])
+
+
 def gelu_cdf(values):
     return 0.5 * (1.0 + jax.scipy.special.erf(values * 0.7071067811865476))
 
@@ -46,7 +422,7 @@
     return placed.reshape(block_count * block_len, width)
 
 
-def body(tokens, assign, gates, cot, w_in, w_out):
+def plain_body(tokens, assign, gates, cot, w_in, w_out):
     own_count = w_in.shape[0]
     block_count = assign.shape[0]
     block_len = tokens.shape[0] // block_count
@@ -56,7 +432,7 @@
         lax.all_gather(w_out, "dp", axis=1, tiled=True),
     )
     expert_ids = lax.axis_index("own") * own_count + jnp.arange(own_count, dtype=jnp.int32)
-    blocks, is_valid = jax.vmap(pick_blocks, (None, 0, None))(assign, expert_ids, CAP)
+    blocks, is_valid = jax.vmap(pick_blocks, (None, 0, None))(assign, expert_ids, CAP)[:2]
     gate_blocks = gates.reshape(block_count, block_len, 2)
     mixing = jax.vmap(block_gates, (None, None, 0, 0, 0))(
         assign, gate_blocks, blocks, is_valid, expert_ids
@@ -112,7 +488,7 @@
         P("own", "dp", None),
     )
     return jax.shard_map(
-        body,
+        functools.partial(body, mesh.shape["dp"]),
         mesh=mesh,
         in_specs=placed,
         out_specs=(P("dp", "own"), P("dp", "own"), P("own", None, "dp"), P("own", "dp", None)),

time: 714 us -> 585 us (0.82)
  waiting for transfers between devices: 516 us -> 115 us
  Pallas kernels: 0 us -> 362 us
  matrix products: 95.1 us -> 0 us
  local copies, waits for them, and re-layouts: 33 us -> 62.7 us
  other arithmetic: 54.4 us -> 29 us
    pallas_call x0 -> x1, Pallas kernels: none -> 362 us  [run_experts(): pl.pallas_call(functools.partial(expert_kernel, chips), out_shape=(jax.Sh...]
    reduce_scatter x2 -> x0, waiting for transfers between devices: 252 us -> none  [the longest x1 129 us: body(): lax.psum_scatter(in_full.astype(jnp.bfloat16), 'dp', scatter_dimension=1,...]
    all_gather x2 -> x0, waiting for transfers between devices: 210 us -> none  [the longest x1 109 us: body(): lax.all_gather(w_in, 'dp', axis=2, tiled=True)]
    dot_general x6 -> x0, matrix products: 95.1 us -> none  [the longest x1 17.5 us: body(): jnp.einsum('erd,efd->erf', grad_out, full_out, preferred_element_type=jnp...]
    unnamed x9 -> x5, waiting for transfers between devices: 15.2 us -> 79.4 us
    scatter-add x2 -> x0, other arithmetic: 35.7 us -> none  [place_rows(): zeros.at[blocks.reshape(-1)].add(terms.reshape(-1, block_len, width))]
    gather x1 -> x5, local copies, waits for them, and re-layouts: 2.9 us -> 19.2 us  [the longest x4 14.4 us: take(): chosen = part.reshape(CAP, block_len, width)[jnp.clip(rank, 0, CAP - 1)]]
    all_gather x1, waiting for transfers between devices: 39.4 us -> 29.7 us  [body(): cot_full = lax.all_gather(cot, 'own', axis=1, tiled=True)]
  transfers between devices with their start and end apart: 7 -> 10, of which waited for: 6 -> 5; matrix products, arithmetic and copies ran while one was open for 17% -> 10% of each run, Pallas kernels for 0% -> 0%
where the time goes in v1:
time: 585 us
  Pallas kernels  362 us (62%)
  waiting for transfers between devices  115 us (20%)
  local copies, waits for them, and re-layouts  62.7 us (11%)
  other arithmetic  29 us (5%)
  between operations  13.9 us (2%)
    pallas_call x1, Pallas kernels, run_experts(): pl.pallas_call(functools.partial(expert_kernel, chips), out_shape=(jax.Sh...  362 us
    unnamed x5, waiting for transfers between devices  79.4 us
    all_gather x1, waiting for transfers between devices, body(): cot_full = lax.all_gather(cot, 'own', axis=1, tiled=True)  29.7 us
    unnamed x25, local copies, waits for them, and re-layouts  21.1 us
    gather x4, local copies, waits for them, and re-layouts, take(): chosen = part.reshape(CAP, block_len, width)[jnp.clip(rank, 0, CAP - 1)]  14.4 us
  transfers between devices with their start and end apart: 10, of which 5 were waited for; matrix products, arithmetic and copies ran while one was open for 10% of the time, Pallas kernels for 0%

profile of v1, /device:TPU:0, one launch (start us, length us, event | category | flops | bytes accessed | tf_op | source)
XLA Modules:
  0.0 584.6 jit_solution(11880593214057111748)
XLA Ops:
  7.2 0.0 copy-start
  7.2 0.0 all-gather.2.cloned.1.call-start
  7.2 0.7 all-gather.2.cloned.1.call-update
  7.9 0.0 reduce-scatter.7.cloned.1.call-start
  8.0 0.8 slice_bitcast_fusion.3
  8.7 0.1 broadcast_compare_fusion
  8.8 0.2 reduce_window_sum.11
  9.0 0.2 convert_reduce_fusion
  9.3 0.1 copy.24
  9.4 0.1 reshape.261
  9.5 4.8 gather_fusion
  14.2 3.7 dynamic-slice_bitcast_fusion.3
  17.9 0.5 collective-permute-start
  18.3 2.7 copy.28
  21.0 3.9 fusion.9
  24.9 0.1 collective-permute-start.3
  25.0 0.1 copy.25
  25.1 0.1 copy.27
  25.2 0.6 gather_fusion.2
  25.7 0.1 copy.26
  25.8 0.1 reshape.276
  25.9 0.6 gather_fusion.1
  26.5 0.1 fusion.13
  26.6 0.1 broadcast_bitcast_fusion
  26.7 0.1 broadcast_bitcast_fusion.1
  26.7 29.7 %all-gather.2.cloned.1.call-done = bf16[1024,1536]{1,0:T(8,128)(2,1)} async-done(((bf16[1024,384]{1,0:T(8,128)(2,1)}), bf16[1024,1536]{1,0:T(8,128)(2,1)}) %all-gather.2.cloned.1.call-update) | async-done | bytes 3145744 | tf_op jit(solution)/shard_map/all_gather | solution.py:372
  56.4 4.8 gather_fusion.3
  61.2 2.8 fusion
  64.0 2.2 dynamic-slice_bitcast_fusion.1
  66.2 0.0 collective-permute-start.1
  66.2 0.6 collective-permute-start.2
  66.8 3.0 collective-permute-done.2
  69.8 1.1 broadcast_in_dim.68.wt_ref
  70.9 0.0 collective-permute-done.3
  70.9 4.8 maximum_select_fusion.own_w
  75.7 3.8 pad_maximum_fusion.x_ref
  79.5 3.7 pad_maximum_fusion.1.g_ref
  83.2 361.7 %shard_map.93 = (bf16[1280,1536]{1,0:T(8,128)(2,1)}, bf16[1280,1536]{1,0:T(8,128)(2,1)}, bf16[2,2,256,1536]{3,2,1,0:T(8,128)(2,1)}) custom-call(bf16[1280,1536]{1,0:T(8,128)(2,1)} %pad_maximum_fusion.x_ref, bf16[1280,1536]{1,0:T(8,128)(2,1)} %pad_maximum_fusion.1.g_ref, f32[1280,1]{1,0:T(8,128)} %broadcast_in_dim.68.wt_ref, ...), custom_call_target="tpu_custom_call" | custom-call | flops 48318382080 | bytes 30000000 | tf_op jit(solution)/shard_map/pallas_call | solution.py:305
  444.9 3.8 fusion.21
  448.7 2.2 fusion.22
  450.9 0.5 collective-permute-start.4
  451.4 0.1 broadcast_bitcast_fusion.3
  451.5 2.4 gather_fusion.6
  453.9 3.9 gather_fusion.4
  457.9 4.0 gather_fusion.7
  461.8 4.1 gather_fusion.5
  466.0 8.6 %fusion.2 = (bf16[1024,1536]{1,0:T(8,128)(2,1)}, bf16[1024,1536]{1,0:T(8,128)(2,1)}) fusion(bf16[8,128,1536]{2,1,0:T(8,128)(2,1)} %gather_fusion.7, bf16[8,128,1536]{2,1,0:T(8,128)(2,1)S(1)} %copy-done.2, pred[1024]{0:T(1024)(128)(4,1)S(1)} %get-tuple-element.62, pred[1024]{0:T(1024)(128)(4,1)S(1)} %get-tuple-element.63, ...), kind=kLoop, calls=%fused_computation.12 | loop fusion | flops 18874368 | bytes 18876416 | tf_op jit(solution)/shard_map/convert_element_type | solution.py:396
  474.6 4.7 copy.31
  479.3 0.0 reduce-scatter.7.cloned.1.call-update
  479.3 0.0 reduce-scatter.9.cloned.1.call-start
  479.3 1.8 copy-done.3
  481.2 2.9 copy.33
  484.1 0.0 reduce-scatter.9.cloned.1.call-update
  484.1 1.9 copy-done.6
  486.0 0.2 constant_dynamic-slice_fusion
  486.2 0.1 collective-permute-start.6
  486.2 3.4 collective-permute-done.6
  489.6 0.7 fusion.5
  490.3 2.1 slice_bitcast_fusion
  492.4 2.4 copy.30
  494.8 34.0 %reduce-scatter.7.cloned.1.call-done = bf16[384,1024]{1,0:T(8,128)(2,1)} async-done(((bf16[1536,1024]{1,0:T(8,128)(2,1)}), bf16[384,1024]{1,0:T(8,128)(2,1)}) %reduce-scatter.7.cloned.1.call-update) | async-done | bytes 786448
  528.8 2.3 copy.32
  531.1 44.7 %reduce-scatter.9.cloned.1.call-done = bf16[384,1024]{1,0:T(8,128)(2,1)} async-done(((bf16[1536,1024]{1,0:T(8,128)(2,1)}), bf16[384,1024]{1,0:T(8,128)(2,1)}) %reduce-scatter.9.cloned.1.call-update) | async-done | bytes 786448
  575.8 2.3 copy.34
  (30 shorter events, 0.2 us)
Async XLA Ops:
  7.2 18.7 %copy-start = (f32[1024,2]{0,1:T(2,128)S(1)}, f32[1024,2]{0,1:T(2,128)}, u32[]{:S(2)}) copy-start(f32[1024,2]{0,1:T(2,128)} %param.8) | copy-start | bytes 24580
  7.2 49.2 %all-gather.2.cloned.1.call-start = ((), (), s32[]{:S(2)}) async-start(), calls=%async_computation.2 | async-start | bytes 3932160 | tf_op jit(solution)/shard_map/all_gather | solution.py:372
  7.9 520.9 %reduce-scatter.7.cloned.1.call-start = ((), (), s32[]{:S(2)}) async-start(), calls=%async_computation.3 | async-start | bytes 3932160
  17.9 57.8 %collective-permute-start = (bf16[640,1536]{1,0:T(8,128)(2,1)}, bf16[640,1536]{1,0:T(8,128)(2,1)}, u32[]{:S(2)}, u32[]{:S(2)}) collective-permute-start(bf16[640,1536]{1,0:T(8,128)(2,1)} %get-tuple-element.43), channel_id=1, source_target_pairs={{0,1},{1,0},{2,3},{3,2},{4,5},{5,4},{6,7},{7,6},{8,9},{9,8},{10,11... | collective-permute-start | bytes 5898248 | tf_op jit(solution)/shard_map/ppermute | solution.py:348
  21.0 4.0 copy-start.7
  24.9 46.0 %collective-permute-start.3 = (bf16[2,256,1536]{2,1,0:T(8,128)(2,1)}, bf16[2,256,1536]{2,1,0:T(8,128)(2,1)}, u32[]{:S(2)}, u32[]{:S(2)}) collective-permute-start(bf16[2,256,1536]{2,1,0:T(8,128)(2,1)} %get-tuple-element.47), channel_id=1, source_target_pairs={{0,1},{1,0},{2,3},{3,2},{4,5},{5,4},{6,7},{7,6},{8,9},{9,8},{10,11... | collective-permute-start | bytes 4718600 | tf_op jit(solution)/shard_map/ppermute | solution.py:348
  66.2 13.3 %collective-permute-start.1 = (bf16[640,1536]{1,0:T(8,128)(2,1)}, bf16[640,1536]{1,0:T(8,128)(2,1)}, u32[]{:S(2)}, u32[]{:S(2)}) collective-permute-start(bf16[640,1536]{1,0:T(8,128)(2,1)} %get-tuple-element.41), channel_id=1, source_target_pairs={{0,1},{1,0},{2,3},{3,2},{4,5},{5,4},{6,7},{7,6},{8,9},{9,8},{10,11... | collective-permute-start | bytes 5898248 | tf_op jit(solution)/shard_map/ppermute | solution.py:348
  66.2 3.6 collective-permute-start.2
  75.7 3.8 copy-start.4
  444.9 3.8 copy-start.5
  448.7 9.2 %collective-permute-start.5 = (bf16[640,1536]{1,0:T(8,128)(2,1)}, bf16[640,1536]{1,0:T(8,128)(2,1)}, u32[]{:S(2)}, u32[]{:S(2)}) collective-permute-start(bf16[640,1536]{1,0:T(8,128)(2,1)} %get-tuple-element.37), channel_id=1, source_target_pairs={{0,1},{1,0},{2,3},{3,2},{4,5},{5,4},{6,7},{7,6},{8,9},{9,8},{10,11... | collective-permute-start | bytes 5898248 | tf_op jit(solution)/shard_map/ppermute | solution.py:348
  450.9 10.9 %collective-permute-start.4 = (bf16[640,1536]{1,0:T(8,128)(2,1)}, bf16[640,1536]{1,0:T(8,128)(2,1)}, u32[]{:S(2)}, u32[]{:S(2)}) collective-permute-start(bf16[640,1536]{1,0:T(8,128)(2,1)} %get-tuple-element.39), channel_id=1, source_target_pairs={{0,1},{1,0},{2,3},{3,2},{4,5},{5,4},{6,7},{7,6},{8,9},{9,8},{10,11... | collective-permute-start | bytes 5898248 | tf_op jit(solution)/shard_map/ppermute | solution.py:348
  461.8 4.1 copy-start.2
  479.3 1.9 copy-start.3
  479.3 96.5 %reduce-scatter.9.cloned.1.call-start = ((), (), s32[]{:S(2)}) async-start(), calls=%async_computation.4 | async-start | bytes 3932160
  484.1 1.9 copy-start.6
  486.2 3.5 collective-permute-start.6
  492.4 85.6 %copy-start.1 = (f32[1024,2]{0,1:T(2,128)S(1)}, f32[1024,2]{0,1:T(2,128)}, u32[]{:S(2)}) copy-start(f32[1024,2]{0,1:T(2,128)} %param.8) | copy-start | bytes 24580
Sparse Core Ops, SparseCore 0:
  9.8 46.5 all-gather.1
  479.4 49.3 reduce-scatter.6
  531.8 43.9 reduce-scatter.8

commit v2 on v1

--- a/solution.py
+++ b/solution.py
@@ -37,13 +37,21 @@
 
 def expert_kernel(
     chips,
+    x_mine,
+    x_theirs,
+    g_mine,
+    g_theirs,
+    wt_ref,
+    w_mine,
+    w_theirs,
+    y_mine,
+    y_theirs,
+    gx_mine,
+    gx_theirs,
+    dw_mine,
+    dw_theirs,
     x_ref,
     g_ref,
-    wt_ref,
-    own_w,
-    y_out,
-    gx_out,
-    dw_out,
     w_all,
     h_all,
     p_all,
@@ -54,12 +62,14 @@
     rs_send,
     rs_recv,
     own_sem,
+    in_sem,
     out_sem,
 ):
     me = lax.axis_index("dp")
-    chip = me // 2
+    chip, core = me // 2, me % 2
     rows, width = x_ref.shape
-    depth = own_w.shape[1] // 2
+    half = rows // 2
+    depth = w_mine.shape[1]
     last = chips - 1
     has_left, has_right = chip > 0, chip < last
 
@@ -86,10 +96,25 @@
             device_id_type=MESH,
         )
 
-    own_copy = pltpu.make_async_copy(
-        own_w, w_all.at[:, pl.ds(pl.multiple_of(chip * 2 * depth, depth), 2 * depth)], own_sem
-    )
-    own_copy.start()
+    own_copies = [
+        pltpu.make_async_copy(src, at_chunk(w_all, 2 * chip + place), own_sem.at[i])
+        for i, (src, place) in enumerate(((w_mine, core), (w_theirs, 1 - core)))
+    ]
+    for copy in own_copies:
+        copy.start()
+    in_copies = [
+        pltpu.make_async_copy(src, dst, in_sem.at[i])
+        for i, (src, dst) in enumerate(
+            (
+                (x_mine, x_ref.at[:half]),
+                (x_theirs, x_ref.at[half:]),
+                (g_mine, g_ref.at[:half]),
+                (g_theirs, g_ref.at[half:]),
+            )
+        )
+    ]
+    for copy in in_copies:
+        copy.start()
     barrier = pltpu.get_barrier_semaphore()
 
     @pl.when(has_left)
@@ -102,7 +127,8 @@
 
     pl.semaphore_wait(barrier, has_left.astype(jnp.int32) + has_right.astype(jnp.int32))
 
-    own_copy.wait()
+    for copy in own_copies:
+        copy.wait()
     for sub in range(2):
 
         @pl.when(has_left)
@@ -113,7 +139,10 @@
         def _():
             gather_copy(2 * chip + sub, 1).start()
 
-    tile = rows // 2
+    for copy in in_copies:
+        copy.wait()
+
+    tile = half
     nt = (((1,), (1,)), ((), ()))
 
     def activate(q):
@@ -208,35 +237,31 @@
 
     lax.fori_loop(0, turns, turn, 0)
 
-    out_tile = rows // 5
-
-    def rows_out(i, carry):
-        part = pl.ds(pl.multiple_of(i * out_tile, out_tile), out_tile)
-
-        def columns(k, inner):
-            span = pl.ds(pl.multiple_of(k * piece, piece), piece)
-            stage[0, :, span] = (
-                jnp.dot(h_all[part, :], w_all[1, :, span], preferred_element_type=jnp.float32)
-                * wt_ref[part, :]
-            ).astype(jnp.bfloat16)
-            stage[1, :, span] = jnp.dot(
-                p_all[part, :], w_all[0, :, span], preferred_element_type=jnp.float32
-            ).astype(jnp.bfloat16)
-            return inner
-
-        lax.fori_loop(0, 3, columns, 0)
-        y_copy = pltpu.make_async_copy(stage.at[0], y_out.at[part], out_sem.at[0])
-        gx_copy = pltpu.make_async_copy(stage.at[1], gx_out.at[part], out_sem.at[1])
+    blocks, columns, block_len, share = y_mine.shape
+
+    for side, (y_out, gx_out) in enumerate(((y_mine, gx_mine), (y_theirs, gx_theirs))):
+        part = pl.ds(side * half, half)
+
+        def column(k, carry):
+            span = pl.ds(pl.multiple_of(k * share, share), share)
+            y = jnp.dot(h_all[part, :], w_all[1, :, span], preferred_element_type=jnp.float32)
+            y = (y * wt_ref[part, :]).astype(jnp.bfloat16)
+            gx = jnp.dot(p_all[part, :], w_all[0, :, span], preferred_element_type=jnp.float32)
+            gx = gx.astype(jnp.bfloat16)
+            for b in range(blocks):
+                stage[0, b, k] = y[b * block_len : (b + 1) * block_len]
+                stage[1, b, k] = gx[b * block_len : (b + 1) * block_len]
+            return carry
+
+        lax.fori_loop(0, columns, column, 0)
+        y_copy = pltpu.make_async_copy(stage.at[0], y_out, out_sem.at[0])
+        gx_copy = pltpu.make_async_copy(stage.at[1], gx_out, out_sem.at[1])
         y_copy.start()
         gx_copy.start()
         y_copy.wait()
         gx_copy.wait()
-        return carry
-
-    lax.fori_loop(0, 5, rows_out, 0)
-
-    def finish(sub, carry):
-        q = 2 * chip + sub
+
+    def finish(q, dw_out):
 
         @pl.when(has_left)
         def _():
@@ -255,16 +280,16 @@
             sums[q] = jnp.zeros(sums.shape[1:], sums.dtype)
 
         def emit(kind, span, value):
-            dw_out[sub, kind, :, span] = (
+            dw_out[kind, :, span] = (
                 value
                 + sums[q, kind, :, span].astype(jnp.float32)
                 + sums[q + 2, kind, :, span].astype(jnp.float32)
             ).astype(jnp.bfloat16)
 
         weight_grads(q, emit)
-        return carry
-
-    lax.fori_loop(0, 2, finish, 0)
+
+    finish(2 * chip + 1 - core, dw_theirs)
+    finish(2 * chip + core, dw_mine)
 
     for sub in range(2):
 
@@ -294,34 +319,36 @@
     lax.fori_loop(0, 2 * last, drain, 0)
 
 
-def run_experts(shards, x, g, weights, own_w):
+def run_experts(shards, owners, x, g, weights, own_w):
     chips = shards // 2
-    rows, width = x.shape
-    depth = own_w.shape[1] // 2
+    half, width = x[0].shape
+    rows = 2 * half
+    depth = own_w[0].shape[1]
     hidden = shards * depth
     slots = shards + 2
     vmem = pl.BlockSpec(memory_space=pltpu.VMEM)
     hbm = pl.BlockSpec(memory_space=pl.ANY)
+    token_out = jax.ShapeDtypeStruct((CAP, owners, half // CAP, width // owners), jnp.bfloat16)
+    weight_out = jax.ShapeDtypeStruct((2, depth, width), jnp.bfloat16)
     return pl.pallas_call(
         functools.partial(expert_kernel, chips),
-        out_shape=(
-            jax.ShapeDtypeStruct((rows, width), jnp.bfloat16),
-            jax.ShapeDtypeStruct((rows, width), jnp.bfloat16),
-            jax.ShapeDtypeStruct((2, 2, depth, width), jnp.bfloat16),
-        ),
-        in_specs=[vmem, vmem, vmem, hbm],
-        out_specs=(hbm, hbm, vmem),
+        out_shape=(token_out,) * 4 + (weight_out,) * 2,
+        in_specs=[hbm] * 4 + [vmem] + [hbm] * 2,
+        out_specs=(hbm,) * 4 + (vmem,) * 2,
         scratch_shapes=[
+            pltpu.VMEM((rows, width), jnp.bfloat16),
+            pltpu.VMEM((rows, width), jnp.bfloat16),
             pltpu.VMEM((2, hidden, width), jnp.bfloat16),
             pltpu.VMEM((rows, hidden), jnp.bfloat16),
             pltpu.VMEM((rows, hidden), jnp.bfloat16),
             pltpu.VMEM((slots, 2, depth, width), jnp.bfloat16),
-            pltpu.VMEM((2, rows // 5, width), jnp.bfloat16),
+            pltpu.VMEM((2,) + token_out.shape, jnp.bfloat16),
             pltpu.SemaphoreType.DMA((shards, 2)),
             pltpu.SemaphoreType.DMA((shards,)),
             pltpu.SemaphoreType.DMA((slots,)),
             pltpu.SemaphoreType.DMA((slots,)),
-            pltpu.SemaphoreType.DMA,
+            pltpu.SemaphoreType.DMA((2,)),
+            pltpu.SemaphoreType.DMA((4,)),
             pltpu.SemaphoreType.DMA((2,)),
         ],
         compiler_params=pltpu.CompilerParams(
@@ -330,10 +357,10 @@
         cost_estimate=pl.CostEstimate(
             flops=12 * rows * width * hidden, bytes_accessed=30_000_000, transcendentals=0
         ),
-    )(x, g, weights, own_w)
-
-
-def body(shards, tokens, assign, gates, cot, w_in, w_out):
+    )(*x, *g, weights, *own_w)
+
+
+def body(shards, owners, tokens, assign, gates, cot, w_in, w_out):
     own_count = w_in.shape[0]
     if own_count != 2:
         return plain_body(tokens, assign, gates, cot, w_in, w_out)
@@ -354,12 +381,7 @@
         return lax.dynamic_index_in_dim(array, 1 - core, 0, keepdims=False)
 
     both = jnp.stack([jnp.transpose(w_in, (0, 2, 1)), w_out], axis=1)
-    kept, got = mine(both), swap(other(both))
-    own_w = jnp.where(
-        core == 0,
-        jnp.concatenate([kept, got], axis=1),
-        jnp.concatenate([got, kept], axis=1),
-    )
+    own_w = (mine(both), swap(other(both)))
     expert_ids = lax.axis_index("own") * own_count + jnp.arange(own_count, dtype=jnp.int32)
     blocks, is_valid, hits, ranks = jax.vmap(pick_blocks, (None, 0, None))(assign, expert_ids, CAP)
     gate_blocks = gates.reshape(block_count, block_len, 2)
@@ -376,29 +398,35 @@
     grad_out = (weight_rows[..., None] * cot_picked.astype(jnp.float32)).astype(jnp.bfloat16)
 
     def shared(array):
-        return jnp.concatenate([mine(array), swap(other(array))], axis=0)
+        return (mine(array), swap(other(array)))
 
     x = shared(picked)
     g = shared(grad_out)
-    weights = shared(weight_rows)[:, None]
-    y, gx, dw = run_experts(shards, x, g, weights, own_w)
+    weights = jnp.concatenate(shared(weight_rows))[:, None]
+    y_mine, y_theirs, gx_mine, gx_theirs, dw_mine, dw_theirs = run_experts(
+        shards, owners, x, g, weights, own_w
+    )
 
     my_hit, my_rank = mine(hits), mine(ranks)
     other_hit, other_rank = other(hits), other(ranks)
 
-    def by_block(array):
+    def by_block(kept, back):
         def take(part, hit, rank):
-            chosen = part.reshape(CAP, block_len, width)[jnp.clip(rank, 0, CAP - 1)]
-            return jnp.where(hit[:, None, None] == 1, chosen.astype(jnp.float32), 0.0)
-
-        back = swap(array[rows:])
-        total = take(array[:rows], my_hit, my_rank) + take(back, other_hit, other_rank)
-        total = total.astype(jnp.bfloat16).reshape(block_count * block_len, width)
-        return lax.psum_scatter(total, "own", scatter_dimension=1, tiled=True)
-
-    mixed = by_block(y)
-    grad_tokens = by_block(gx)
-    dw_kept, dw_got = mine(dw), swap(other(dw))
+            chosen = part[jnp.clip(rank, 0, CAP - 1)]
+            return jnp.where(hit[:, None, None, None] == 1, chosen.astype(jnp.float32), 0.0)
+
+        total = take(kept, my_hit, my_rank) + take(back, other_hit, other_rank)
+        total = jnp.swapaxes(total.astype(jnp.bfloat16), 0, 1)
+        return total.reshape(owners, block_count * block_len, width // owners)
+
+    y_back, gx_back, dw_got = swap(y_theirs), swap(gx_theirs), swap(dw_theirs)
+    y_total = by_block(y_mine, y_back)
+    y_total, gx_mine, gx_back = lax.optimization_barrier((y_total, gx_mine, gx_back))
+    mixed = lax.psum_scatter(y_total, "own", scatter_dimension=0, tiled=False)
+    grad_tokens = lax.psum_scatter(
+        by_block(gx_mine, gx_back), "own", scatter_dimension=0, tiled=False
+    )
+    dw_kept = dw_mine
     dw_all = jnp.where(
         core == 0, jnp.stack([dw_kept, dw_got]), jnp.stack([dw_got, dw_kept])
     ).astype(jnp.float32)
@@ -488,7 +516,7 @@
         P("own", "dp", None),
     )
     return jax.shard_map(
-        functools.partial(body, mesh.shape["dp"]),
+        functools.partial(body, mesh.shape["dp"], mesh.shape["own"]),
         mesh=mesh,
         in_specs=placed,
         out_specs=(P("dp", "own"), P("dp", "own"), P("own", None, "dp"), P("own", "dp", None)),

time: 585 us -> 573 us (0.979)
  local copies, waits for them, and re-layouts: 62.7 us -> 44.7 us
  waiting for transfers between devices: 115 us -> 133 us
  other arithmetic: 29 us -> 13.8 us
    unnamed x25 -> x15, local copies, waits for them, and re-layouts: 21.1 us -> 5.44 us
    unnamed x5, waiting for transfers between devices: 79.4 us -> 88.9 us
    concatenate x3 -> x1, other arithmetic: 7.46 us -> 0.01 us  [body(): weights = jnp.concatenate(shared(weight_rows))[:, None]]
    all_gather x1, waiting for transfers between devices: 29.7 us -> 36.2 us  [body(): cot_full = lax.all_gather(cot, 'own', axis=1, tiled=True)]
    slice x2 -> x0, local copies, waits for them, and re-layouts: 5.99 us -> none  [by_block(): array[:rows]]
  transfers between devices with their start and end apart: 10 -> 10, of which waited for: 5 -> 6; matrix products, arithmetic and copies ran while one was open for 10% -> 8% of each run, Pallas kernels for 0% -> 0%
where the time goes in v2:
time: 573 us; the launch traced here: 572 us
  Pallas kernels  365 us (64%)
  waiting for transfers between devices  133 us (23%)
  local copies, waits for them, and re-layouts  44.7 us (8%)
  between operations  13.9 us (2%)
  other arithmetic  13.8 us (2%)
    pallas_call x1, Pallas kernels, run_experts(): pl.pallas_call(functools.partial(expert_kernel, chips), out_shape=(token_...  365 us
    unnamed x5, waiting for transfers between devices  88.9 us
    all_gather x1, waiting for transfers between devices, body(): cot_full = lax.all_gather(cot, 'own', axis=1, tiled=True)  36.2 us
    gather x4, local copies, waits for them, and re-layouts, take(): chosen = part[jnp.clip(rank, 0, CAP - 1)]  14 us
  transfers between devices with their start and end apart: 10, of which 6 were waited for; matrix products, arithmetic and copies ran while one was open for 8% of the time, Pallas kernels for 0%

profile of v2, /device:TPU:0, one launch (start us, length us, event | category | flops | bytes accessed | tf_op | source)
XLA Modules:
  0.0 572.0 jit_solution(764722821903648604)
XLA Ops:
  7.2 0.0 copy-start
  7.2 0.0 all-gather.2.cloned.1.call-start
  7.2 0.7 all-gather.2.cloned.1.call-update
  7.9 0.0 reduce-scatter.9.cloned.1.call-start
  8.0 0.8 slice_bitcast_fusion.3
  8.8 0.1 broadcast_compare_fusion
  8.8 0.2 reduce_window_sum.11
  9.0 0.2 convert_reduce_fusion
  9.3 0.1 copy.28
  9.4 0.1 reshape.231
  9.5 4.9 gather_fusion
  14.3 3.7 dynamic-slice_bitcast_fusion.2
  18.0 0.5 collective-permute-start
  18.5 0.0 copy-done.3
  18.5 0.1 copy.29
  18.5 0.6 gather_fusion.2
  19.1 0.1 copy.30
  19.2 0.1 reshape.246
  19.3 0.0 copy-done
  19.3 0.6 gather_fusion.1
  19.9 0.1 copy.31
  20.0 0.1 fusion.11
  20.1 0.1 broadcast_bitcast_fusion
  20.1 0.1 broadcast_bitcast_fusion.1
  20.2 36.2 %all-gather.2.cloned.1.call-done = bf16[1024,1536]{1,0:T(8,128)(2,1)} async-done(((bf16[1024,384]{1,0:T(8,128)(2,1)}), bf16[1024,1536]{1,0:T(8,128)(2,1)}) %all-gather.2.cloned.1.call-update) | async-done | bytes 3145744 | tf_op jit(solution)/shard_map/all_gather | solution.py:394
  56.5 4.9 gather_fusion.3
  61.3 2.8 fusion
  64.1 2.2 dynamic-slice_bitcast_fusion
  66.3 0.0 collective-permute-start.1
  66.3 1.7 copy.32
  68.0 2.8 fusion.5
  70.9 0.5 collective-permute-start.3
  71.4 0.1 collective-permute-start.2
  71.5 2.9 collective-permute-done.2
  74.4 1.1 broadcast_in_dim.56.wt_ref
  75.5 0.0 collective-permute-done.3.w_theirs
  75.5 0.0 collective-permute-done.x_theirs
  75.5 1.1 copy-done.4
  76.7 0.0 collective-permute-done.1.g_theirs
  76.7 365.0 %shard_map.93 = (bf16[5,4,128,384]{3,2,1,0:T(8,128)(2,1)}, bf16[5,4,128,384]{3,2,1,0:T(8,128)(2,1)}, bf16[5,4,128,384]{3,2,1,0:T(8,128)(2,1)}, bf16[5,4,128,384]...) custom-call(bf16[640,1536]{1,0:T(8,128)(2,1)} %get-tuple-element.51.x_mine, ...), custom_call_target="tpu_custom_call" | custom-call | flops 48318382080 | bytes 30000000 | tf_op jit(solution)/shard_map/pallas_call | solution.py:333
  441.7 0.1 collective-permute-start.4
  441.8 0.5 collective-permute-start.5
  442.3 2.8 gather_fusion.4
  445.1 1.0 collective-permute-done.4
  446.1 4.2 gather_fusion.5
  450.3 3.5 fusion.1
  453.8 2.1 copy.34
  455.9 0.0 collective-permute-done.5
  455.9 2.8 gather_fusion.6
  458.7 4.2 gather_fusion.7
  462.9 3.5 fusion.2
  466.3 2.1 copy.35
  468.4 0.0 reduce-scatter.9.cloned.1.call-update
  468.5 0.0 reduce-scatter.7.cloned.1.call-start
  468.5 0.7 reduce-scatter.7.cloned.1.call-update
  469.2 0.2 collective-permute-start.6
  469.4 3.5 collective-permute-done.6
  472.9 0.0 copy-done.2
  472.9 0.6 fusion.3
  473.5 2.1 slice_bitcast_fusion
  475.6 2.4 copy.36
  477.9 40.0 %reduce-scatter.9.cloned.1.call-done = bf16[1,1024,384]{2,1,0:T(8,128)(2,1)} async-done(((bf16[4,1024,384]{2,1,0:T(8,128)(2,1)}), bf16[1,1024,384]{2,1,0:T(8,128)(2,1)}) %reduce-scatter.9.cloned.1.call-update) | async-done | bytes 786448
  517.9 47.5 %reduce-scatter.7.cloned.1.call-done = bf16[1,1024,384]{2,1,0:T(8,128)(2,1)} async-done(((bf16[4,1024,384]{2,1,0:T(8,128)(2,1)}), bf16[1,1024,384]{2,1,0:T(8,128)(2,1)}) %reduce-scatter.7.cloned.1.call-update) | async-done | bytes 786448
  565.5 0.0 copy-done.1
  (16 shorter events, 0.1 us)
Async XLA Ops:
  7.2 12.1 %copy-start = (f32[1024,2]{0,1:T(2,128)S(1)}, f32[1024,2]{0,1:T(2,128)}, u32[]{:S(2)}) copy-start(f32[1024,2]{0,1:T(2,128)} %param.8) | copy-start | bytes 24580
  7.2 49.3 %all-gather.2.cloned.1.call-start = ((), (), s32[]{:S(2)}) async-start(), calls=%async_computation.2 | async-start | bytes 3932160 | tf_op jit(solution)/shard_map/all_gather | solution.py:394
  7.9 510.0 %reduce-scatter.9.cloned.1.call-start = ((), (), s32[]{:S(2)}) async-start(), calls=%async_computation.4 | async-start | bytes 3932160
  14.3 4.1 copy-start.3
  18.0 57.5 %collective-permute-start = (bf16[640,1536]{1,0:T(8,128)(2,1)S(1)}, bf16[640,1536]{1,0:T(8,128)(2,1)}, u32[]{:S(2)}, u32[]{:S(2)}) collective-permute-start(bf16[640,1536]{1,0:T(8,128)(2,1)S(1)} %get-tuple-element.50), channel_id=1, source_target_pairs={{0,1},{1,0},{2,3},{3,2},{4,5},{5,4},{6,7},{7,6},{8,9},{9,8},{10,11... | collective-permute-start | bytes 5898248 | tf_op jit(solution)/shard_map/ppermute | solution.py:375
  66.3 10.3 %collective-permute-start.1 = (bf16[640,1536]{1,0:T(8,128)(2,1)}, bf16[640,1536]{1,0:T(8,128)(2,1)}, u32[]{:S(2)}, u32[]{:S(2)}) collective-permute-start(bf16[640,1536]{1,0:T(8,128)(2,1)} %get-tuple-element.48), channel_id=1, source_target_pairs={{0,1},{1,0},{2,3},{3,2},{4,5},{5,4},{6,7},{7,6},{8,9},{9,8},{10,11... | collective-permute-start | bytes 5898248 | tf_op jit(solution)/shard_map/ppermute | solution.py:375
  70.9 4.6 collective-permute-start.3
  71.4 3.0 collective-permute-start.2
  75.5 1.1 copy-start.4
  441.7 4.4 collective-permute-start.4
  441.8 14.1 %collective-permute-start.5 = (bf16[5,4,128,384]{3,2,1,0:T(8,128)(2,1)}, bf16[5,4,128,384]{3,2,1,0:T(8,128)(2,1)}, u32[]{:S(2)}, u32[]{:S(2)}) collective-permute-start(bf16[5,4,128,384]{3,2,1,0:T(8,128)(2,1)} %get-tuple-element.16), channel_id=1, source_target_pairs={{0,1},{1,0},{2,3},{3,2},{4,5},{5,4},{6,7},{7,6},{8,9},{9,8},{10,11... | collective-permute-start | bytes 5898248 | tf_op jit(solution)/shard_map/ppermute | solution.py:375
  468.4 4.5 copy-start.2
  468.5 97.0 %reduce-scatter.7.cloned.1.call-start = ((), (), s32[]{:S(2)}) async-start(), calls=%async_computation.3 | async-start | bytes 3932160
  469.2 3.7 collective-permute-start.6
  475.6 89.9 %copy-start.1 = (f32[1024,2]{0,1:T(2,128)S(1)}, f32[1024,2]{0,1:T(2,128)}, u32[]{:S(2)}) copy-start(f32[1024,2]{0,1:T(2,128)} %param.8) | copy-start | bytes 24580
Sparse Core Ops, SparseCore 0:
  9.8 46.5 all-gather.1
  468.6 49.3 reduce-scatter.8
  521.5 43.9 reduce-scatter.6

commit v3 on v2

--- a/solution.py
+++ b/solution.py
@@ -374,6 +374,11 @@
     def swap(array):
         return lax.ppermute(array, "dp", pairs)
 
+    owner = lax.axis_index("own")
+
+    def exchange(array, step):
+        return lax.ppermute(array, "own", [(i, i ^ step) for i in range(owners)])
+
     def mine(array):
         return lax.dynamic_index_in_dim(array, core, 0, keepdims=False)
 
@@ -391,7 +396,12 @@
     weight_rows = mixing.reshape(own_count, rows)
     token_blocks = tokens.reshape(block_count, block_len, width)
     picked = token_blocks[blocks].reshape(own_count, rows, width)
-    cot_full = lax.all_gather(cot, "own", axis=1, tiled=True)
+    cot_full = jnp.zeros((cot.shape[0], width), cot.dtype)
+    for step in range(owners):
+        part = exchange(cot, step) if step else cot
+        cot_full = lax.dynamic_update_slice_in_dim(
+            cot_full, part, (owner ^ step) * cot.shape[1], axis=1
+        )
     cot_picked = cot_full.reshape(block_count, block_len, width)[blocks].reshape(
         own_count, rows, width
     )
@@ -416,16 +426,20 @@
             return jnp.where(hit[:, None, None, None] == 1, chosen.astype(jnp.float32), 0.0)
 
         total = take(kept, my_hit, my_rank) + take(back, other_hit, other_rank)
-        total = jnp.swapaxes(total.astype(jnp.bfloat16), 0, 1)
-        return total.reshape(owners, block_count * block_len, width // owners)
+        total = total.astype(jnp.bfloat16).reshape(block_count, owners, block_len, width // owners)
+
+        def chunk(step):
+            return lax.dynamic_index_in_dim(total, owner ^ step, 1, keepdims=False)
+
+        received = [exchange(chunk(step), step) for step in range(1, owners)]
+        summed = chunk(0).astype(jnp.float32)
+        for part in received:
+            summed = summed + part.astype(jnp.float32)
+        return summed.astype(jnp.bfloat16).reshape(block_count * block_len, width // owners)
 
     y_back, gx_back, dw_got = swap(y_theirs), swap(gx_theirs), swap(dw_theirs)
-    y_total = by_block(y_mine, y_back)
-    y_total, gx_mine, gx_back = lax.optimization_barrier((y_total, gx_mine, gx_back))
-    mixed = lax.psum_scatter(y_total, "own", scatter_dimension=0, tiled=False)
-    grad_tokens = lax.psum_scatter(
-        by_block(gx_mine, gx_back), "own", scatter_dimension=0, tiled=False
-    )
+    mixed = by_block(y_mine, y_back)
+    grad_tokens = by_block(gx_mine, gx_back)
     dw_kept = dw_mine
     dw_all = jnp.where(
         core == 0, jnp.stack([dw_kept, dw_got]), jnp.stack([dw_got, dw_kept])

time: 573 us -> 533 us (0.930)
  waiting for transfers between devices: 133 us -> 73.9 us
  between operations: 13.9 us -> 0.87 us
  starting transfers between devices: 1.92 us -> 13.8 us
  other arithmetic: 13.8 us -> 22.3 us
  local copies, waits for them, and re-layouts: 44.7 us -> 52.2 us
    unnamed x5 -> x0, waiting for transfers between devices: 88.9 us -> none
    ppermute x0 -> x9, waiting for transfers between devices: none -> 70.9 us  [exchange(): return lax.ppermute(array, 'own', [(i, i ^ step) for i in range(owners)])]
    all_gather x1 -> x0, waiting for transfers between devices: 36.2 us -> none  [body(): cot_full = lax.all_gather(cot, 'own', axis=1, tiled=True)]
    ppermute x0 -> x9, starting transfers between devices: none -> 12.6 us  [exchange(): return lax.ppermute(array, 'own', [(i, i ^ step) for i in range(owners)])]
    convert_element_type x2 -> x3, other arithmetic: 6.93 us -> 12.6 us  [the longest x1 6.44 us: by_block(): total.astype(jnp.bfloat16)]
  transfers between devices with their start and end apart: 10 -> 16, of which waited for: 6 -> 7; matrix products, arithmetic and copies ran while one was open for 8% -> 13% of each run, Pallas kernels for 0% -> 0%
where the time goes in v3:
time: 533 us; the launch traced here: 528 us
  Pallas kernels  365 us (68%)
  waiting for transfers between devices  73.9 us (14%)
  local copies, waits for them, and re-layouts  52.2 us (10%)
  other arithmetic  22.3 us (4%)
  starting transfers between devices  13.8 us (3%)
    pallas_call x1, Pallas kernels, run_experts(): pl.pallas_call(functools.partial(expert_kernel, chips), out_shape=(token_...  365 us
    ppermute x9, waiting for transfers between devices, exchange(): return lax.ppermute(array, 'own', [(i, i ^ step) for i in range(owners)])  70.9 us
    gather x4, local copies, waits for them, and re-layouts, take(): chosen = part[jnp.clip(rank, 0, CAP - 1)]  15.4 us
    ppermute x9, starting transfers between devices, exchange(): return lax.ppermute(array, 'own', [(i, i ^ step) for i in range(owners)])  12.6 us
  transfers between devices with their start and end apart: 16, of which 7 were waited for; matrix products, arithmetic and copies ran while one was open for 13% of the time, Pallas kernels for 0%

profile of v3, /device:TPU:0, one launch (start us, length us, event | category | flops | bytes accessed | tf_op | source)
XLA Modules:
  0.0 528.4 jit_solution(8826068231242531771)
XLA Ops:
  0.6 0.0 copy-start
  0.6 3.0 collective-permute-start.1
  3.7 1.5 collective-permute-start.2
  5.2 0.0 collective-permute-start.3
  5.2 0.8 slice_bitcast_fusion.3
  6.0 0.1 broadcast_compare_fusion
  6.0 0.2 reduce_window_sum.11
  6.2 0.2 convert_reduce_fusion
  6.5 0.1 copy.19
  6.6 0.1 reshape.237
  6.7 4.8 gather_fusion
  11.5 4.3 dynamic-slice_bitcast_fusion.2
  15.8 0.1 copy.20
  15.9 0.6 gather_fusion.2
  16.4 0.1 copy.21
  16.5 0.1 reshape.252
  16.6 0.1 copy.22
  16.7 0.1 broadcast_bitcast_fusion
  16.8 0.1 fusion.15
  16.8 0.6 gather_fusion.1
  17.4 0.2 broadcast_in_dim.31
  17.7 1.3 constant_dynamic-update-slice_fusion.3
  19.0 0.1 broadcast_bitcast_fusion.1
  19.1 3.3 collective-permute-done.1
  22.3 1.3 constant_dynamic-update-slice_fusion.2
  23.6 16.2 %collective-permute-done.2 = bf16[1024,384]{1,0:T(8,128)(2,1)} collective-permute-done((bf16[1024,384]{1,0:T(8,128)(2,1)}, bf16[1024,384]{1,0:T(8,128)(2,1)}, u32[]{:S(2)}, u32[]{:S(2)}) %collective-permute-start.2) | collective-permute-done | bytes 786464 | tf_op jit(solution)/shard_map/ppermute | solution.py:380
  39.8 1.3 constant_dynamic-update-slice_fusion.1
  41.1 1.3 constant_dynamic-update-slice_fusion
  42.4 2.9 gather_fusion.3
  45.3 2.8 fusion
  48.1 1.5 dynamic-slice_bitcast_fusion
  49.7 1.7 copy.23
  51.4 2.8 fusion.3
  54.2 0.5 collective-permute-start.6
  54.8 0.1 collective-permute-start.5
  54.9 2.9 collective-permute-done.5
  57.8 1.1 broadcast_in_dim.60.wt_ref
  58.9 1.1 copy-done.5
  60.0 365.3 %shard_map.93 = (bf16[5,4,128,384]{3,2,1,0:T(8,128)(2,1)}, bf16[5,4,128,384]{3,2,1,0:T(8,128)(2,1)}, bf16[5,4,128,384]{3,2,1,0:T(8,128)(2,1)}, bf16[5,4,128,384]...) custom-call(bf16[640,1536]{1,0:T(8,128)(2,1)} %get-tuple-element.41.x_mine, ...), custom_call_target="tpu_custom_call" | custom-call | flops 48318382080 | bytes 30000000 | tf_op jit(solution)/shard_map/pallas_call | solution.py:333
  425.4 0.1 collective-permute-start.7
  425.4 0.5 collective-permute-start.11
  425.9 0.1 collective-permute-start.15
  426.1 2.8 gather_fusion.4
  428.9 4.2 gather_fusion.6
  433.1 4.2 gather_fusion.5
  437.3 4.2 gather_fusion.7
  441.5 6.4 %add_convert_fusion = (bf16[8,4,128,384]{3,2,1,0:T(8,128)(2,1)S(1)}, bf16[8,4,128,384]{3,2,1,0:T(8,128)(2,1)}) fusion(bf16[8,4,128,384]{3,2,1,0:T(8,128)(2,1)} %gather_fusion.7, bf16[8,4,128,384]{3,2,1,0:T(8,128)(2,1)} %gather_fusion.6, pred[8]{0:T(512)(128)(4,1)S(1)} %get-tuple-element.55, pred[8]{0:T(512)(128)(4,1)S(1)} %get-tuple-element.54, ...), kind=kLoop, calls=%fused_computation.10 | loop fusion | flops 18874368 | bytes 18874384 | tf_op jit(solution)/shard_map/convert_element_type | solution.py:429
  447.9 1.6 copy-done.3
  449.6 1.5 dynamic-slice_bitcast_fusion.6
  451.1 3.4 fusion.1
  454.5 2.1 collective-permute-start.13
  456.7 1.4 collective-permute-start.14
  458.1 1.5 dynamic-slice_bitcast_fusion.9
  459.6 1.5 collective-permute-start.10
  461.1 1.5 collective-permute-start.8
  462.6 9.2 %collective-permute-done.12 = bf16[8,128,384]{2,1,0:T(8,128)(2,1)} collective-permute-done((bf16[8,128,384]{2,1,0:T(8,128)(2,1)}, bf16[8,128,384]{2,1,0:T(8,128)(2,1)}, u32[]{:S(2)}, u32[]{:S(2)}) %collective-permute-start.12) | collective-permute-done | bytes 786464 | tf_op jit(solution)/shard_map/ppermute | solution.py:380
  471.8 1.5 collective-permute-start.9
  473.3 3.2 slice_bitcast_fusion
  476.5 3.6 copy.25
  480.0 29.0 %collective-permute-done.13 = bf16[8,128,384]{2,1,0:T(8,128)(2,1)} collective-permute-done((bf16[8,128,384]{2,1,0:T(8,128)(2,1)}, bf16[8,128,384]{2,1,0:T(8,128)(2,1)}, u32[]{:S(2)}, u32[]{:S(2)}) %collective-permute-start.13) | collective-permute-done | bytes 786464 | tf_op jit(solution)/shard_map/ppermute | solution.py:380
  509.0 3.1 fusion.8
  512.2 9.8 %collective-permute-done.8 = bf16[8,128,384]{2,1,0:T(8,128)(2,1)} collective-permute-done((bf16[8,128,384]{2,1,0:T(8,128)(2,1)}, bf16[8,128,384]{2,1,0:T(8,128)(2,1)}, u32[]{:S(2)}, u32[]{:S(2)}) %collective-permute-start.8) | collective-permute-done | bytes 786464 | tf_op jit(solution)/shard_map/ppermute | solution.py:380
  521.9 3.5 collective-permute-done.9
  525.4 3.0 fusion.11
  (33 shorter events, 0.2 us)
Async XLA Ops:
  0.6 16.2 %copy-start = (f32[1024,2]{0,1:T(2,128)S(1)}, f32[1024,2]{0,1:T(2,128)}, u32[]{:S(2)}) copy-start(f32[1024,2]{0,1:T(2,128)} %param.8) | copy-start | bytes 24580
  0.6 21.7 %collective-permute-start.1 = (bf16[1024,384]{1,0:T(8,128)(2,1)}, bf16[1024,384]{1,0:T(8,128)(2,1)}, u32[]{:S(2)}, u32[]{:S(2)}) collective-permute-start(bf16[1024,384]{1,0:T(8,128)(2,1)} %param.9), channel_id=1, source_target_pairs={{0,8},{8,0},{16,24},{24,16},{1,9},{9,1},{17,25},{25,17},{2,10},{10... | collective-permute-start | bytes 2359304 | tf_op jit(solution)/shard_map/ppermute | solution.py:380
  3.7 36.2 %collective-permute-start.2 = (bf16[1024,384]{1,0:T(8,128)(2,1)}, bf16[1024,384]{1,0:T(8,128)(2,1)}, u32[]{:S(2)}, u32[]{:S(2)}) collective-permute-start(bf16[1024,384]{1,0:T(8,128)(2,1)} %param.9), channel_id=1, source_target_pairs={{0,16},{8,24},{16,0},{24,8},{1,17},{9,25},{17,1},{25,9},{2,18},{10... | collective-permute-start | bytes 2359304 | tf_op jit(solution)/shard_map/ppermute | solution.py:380
  5.2 36.0 %collective-permute-start.3 = (bf16[1024,384]{1,0:T(8,128)(2,1)}, bf16[1024,384]{1,0:T(8,128)(2,1)}, u32[]{:S(2)}, u32[]{:S(2)}) collective-permute-start(bf16[1024,384]{1,0:T(8,128)(2,1)} %param.9), channel_id=1, source_target_pairs={{0,24},{8,16},{16,8},{24,0},{1,25},{9,17},{17,9},{25,1},{2,26},{10... | collective-permute-start | bytes 2359304 | tf_op jit(solution)/shard_map/ppermute | solution.py:380
  11.5 4.3 copy-start.4
  15.8 43.1 %collective-permute-start = (bf16[640,1536]{1,0:T(8,128)(2,1)}, bf16[640,1536]{1,0:T(8,128)(2,1)}, u32[]{:S(2)}, u32[]{:S(2)}) collective-permute-start(bf16[640,1536]{1,0:T(8,128)(2,1)} %get-tuple-element.40), channel_id=1, source_target_pairs={{0,1},{1,0},{2,3},{3,2},{4,5},{5,4},{6,7},{7,6},{8,9},{9,8},{10,11... | collective-permute-start | bytes 5898248 | tf_op jit(solution)/shard_map/ppermute | solution.py:375
  49.7 9.2 %collective-permute-start.4 = (bf16[640,1536]{1,0:T(8,128)(2,1)S(1)}, bf16[640,1536]{1,0:T(8,128)(2,1)}, u32[]{:S(2)}, u32[]{:S(2)}) collective-permute-start(bf16[640,1536]{1,0:T(8,128)(2,1)S(1)} %get-tuple-element.38), channel_id=1, source_target_pairs={{0,1},{1,0},{2,3},{3,2},{4,5},{5,4},{6,7},{7,6},{8,9},{9,8},{10,11... | collective-permute-start | bytes 5898248 | tf_op jit(solution)/shard_map/ppermute | solution.py:375
  54.2 4.6 collective-permute-start.6
  54.8 3.0 collective-permute-start.5
  58.9 1.2 copy-start.5
  425.4 7.7 %collective-permute-start.7 = (bf16[5,4,128,384]{3,2,1,0:T(8,128)(2,1)}, bf16[5,4,128,384]{3,2,1,0:T(8,128)(2,1)}, u32[]{:S(2)}, u32[]{:S(2)}) collective-permute-start(bf16[5,4,128,384]{3,2,1,0:T(8,128)(2,1)} %get-tuple-element.11), channel_id=1, source_target_pairs={{0,1},{1,0},{2,3},{3,2},{4,5},{5,4},{6,7},{7,6},{8,9},{9,8},{10,11... | collective-permute-start | bytes 5898248 | tf_op jit(solution)/shard_map/ppermute | solution.py:375
  425.4 11.8 %collective-permute-start.11 = (bf16[5,4,128,384]{3,2,1,0:T(8,128)(2,1)}, bf16[5,4,128,384]{3,2,1,0:T(8,128)(2,1)}, u32[]{:S(2)}, u32[]{:S(2)}) collective-permute-start(bf16[5,4,128,384]{3,2,1,0:T(8,128)(2,1)} %get-tuple-element.13), channel_id=1, source_target_pairs={{0,1},{1,0},{2,3},{3,2},{4,5},{5,4},{6,7},{7,6},{8,9},{9,8},{10,11... | collective-permute-start | bytes 5898248 | tf_op jit(solution)/shard_map/ppermute | solution.py:375
  425.9 25.2 %collective-permute-start.15 = (bf16[2,256,1536]{2,1,0:T(8,128)(2,1)}, bf16[2,256,1536]{2,1,0:T(8,128)(2,1)}, u32[]{:S(2)}, u32[]{:S(2)}) collective-permute-start(bf16[2,256,1536]{2,1,0:T(8,128)(2,1)} %get-tuple-element.15), channel_id=1, source_target_pairs={{0,1},{1,0},{2,3},{3,2},{4,5},{5,4},{6,7},{7,6},{8,9},{9,8},{10,11... | collective-permute-start | bytes 4718600 | tf_op jit(solution)/shard_map/ppermute | solution.py:375
  447.9 1.6 copy-start.3
  451.1 20.7 %collective-permute-start.12 = (bf16[8,128,384]{2,1,0:T(8,128)(2,1)}, bf16[8,128,384]{2,1,0:T(8,128)(2,1)}, u32[]{:S(2)}, u32[]{:S(2)}) collective-permute-start(bf16[8,128,384]{2,1,0:T(8,128)(2,1)} %get-tuple-element.42), channel_id=1, source_target_pairs={{0,8},{8,0},{16,24},{24,16},{1,9},{9,1},{17,25},{25,17},{2,10},{10... | collective-permute-start | bytes 2359304 | tf_op jit(solution)/shard_map/ppermute | solution.py:380
  451.1 7.0 %copy-start.2 = (bf16[8,4,128,384]{3,2,1,0:T(8,128)(2,1)S(1)}, bf16[8,4,128,384]{3,2,1,0:T(8,128)(2,1)}, u32[]{:S(2)}) copy-start(bf16[8,4,128,384]{3,2,1,0:T(8,128)(2,1)} %get-tuple-element.53) | copy-start | bytes 9437188
  454.5 54.5 %collective-permute-start.13 = (bf16[8,128,384]{2,1,0:T(8,128)(2,1)}, bf16[8,128,384]{2,1,0:T(8,128)(2,1)}, u32[]{:S(2)}, u32[]{:S(2)}) collective-permute-start(bf16[8,128,384]{2,1,0:T(8,128)(2,1)} %get-tuple-element.44), channel_id=1, source_target_pairs={{0,16},{8,24},{16,0},{24,8},{1,17},{9,25},{17,1},{25,9},{2,18},{10... | collective-permute-start | bytes 2359304 | tf_op jit(solution)/shard_map/ppermute | solution.py:380
  456.7 52.3 %collective-permute-start.14 = (bf16[8,128,384]{2,1,0:T(8,128)(2,1)}, bf16[8,128,384]{2,1,0:T(8,128)(2,1)}, u32[]{:S(2)}, u32[]{:S(2)}) collective-permute-start(bf16[8,128,384]{2,1,0:T(8,128)(2,1)} %get-tuple-element.43), channel_id=1, source_target_pairs={{0,24},{8,16},{16,8},{24,0},{1,25},{9,17},{17,9},{25,1},{2,26},{10... | collective-permute-start | bytes 2359304 | tf_op jit(solution)/shard_map/ppermute | solution.py:380
  459.6 52.6 %collective-permute-start.10 = (bf16[8,128,384]{2,1,0:T(8,128)(2,1)}, bf16[8,128,384]{2,1,0:T(8,128)(2,1)}, u32[]{:S(2)}, u32[]{:S(2)}) collective-permute-start(bf16[8,128,384]{2,1,0:T(8,128)(2,1)} %get-tuple-element.46), channel_id=1, source_target_pairs={{0,24},{8,16},{16,8},{24,0},{1,25},{9,17},{17,9},{25,1},{2,26},{10... | collective-permute-start | bytes 2359304 | tf_op jit(solution)/shard_map/ppermute | solution.py:380
  461.1 60.8 %collective-permute-start.8 = (bf16[8,128,384]{2,1,0:T(8,128)(2,1)}, bf16[8,128,384]{2,1,0:T(8,128)(2,1)}, u32[]{:S(2)}, u32[]{:S(2)}) collective-permute-start(bf16[8,128,384]{2,1,0:T(8,128)(2,1)} %get-tuple-element.45), channel_id=1, source_target_pairs={{0,8},{8,0},{16,24},{24,16},{1,9},{9,1},{17,25},{25,17},{2,10},{10... | collective-permute-start | bytes 2359304 | tf_op jit(solution)/shard_map/ppermute | solution.py:380
  471.8 53.7 %collective-permute-start.9 = (bf16[8,128,384]{2,1,0:T(8,128)(2,1)}, bf16[8,128,384]{2,1,0:T(8,128)(2,1)}, u32[]{:S(2)}, u32[]{:S(2)}) collective-permute-start(bf16[8,128,384]{2,1,0:T(8,128)(2,1)} %get-tuple-element.47), channel_id=1, source_target_pairs={{0,16},{8,24},{16,0},{24,8},{1,17},{9,25},{17,1},{25,9},{2,18},{10... | collective-permute-start | bytes 2359304 | tf_op jit(solution)/shard_map/ppermute | solution.py:380
  476.5 51.9 %copy-start.1 = (f32[1024,2]{0,1:T(2,128)S(1)}, f32[1024,2]{0,1:T(2,128)}, u32[]{:S(2)}) copy-start(f32[1024,2]{0,1:T(2,128)} %param.8) | copy-start | bytes 24580
